TPU v7x, 32 devices: a whole 2x2x4 slice. The times are simulated.
32 devices in a mesh: section: 16 (over z, y, x), rep: 2 (over core).
Axes of the slice: x: 2, y: 2, z: 4, core: 2. Of those that a mesh axis runs over, the one named last changes fastest.
Arguments:
- features: bfloat16 [4096, 512], P(('section', 'rep')), may hold values from -6 to 6
- col_panels: int32 [32, 2, 12], P('section', 'rep'), may hold values from 0 to 31, as said below
- block_counts: int32 [32, 2], P('section', 'rep'), may hold values from 1 to 12, as said below
- block_values: bfloat16 [32, 2, 12, 128, 128], P('section', 'rep'), may hold values from 0.0019989014 to 0.019897461
- weight: bfloat16 [512, 512], replicated, may hold values from -0.25 to 0.25
- bias: float32 [512], replicated, may hold values from -3 to 3
- cotangent: bfloat16 [4096, 512], P(('section', 'rep')), may hold values from -6 to 6
Outputs:
- hidden: bfloat16 [4096, 512], P(('section', 'rep'))
- weight_grad: float32 [512, 512], replicated
- bias_grad: float32 [512], replicated
Inputs may be any that keep to these rules, and one draw needn't show every extreme that they name: Column group r holds the column panels c with (c) % 2 == r; col_panels[p, r, k] lies in column group r, and the 12 entries of one list are distinct. Only the first block_counts[p, r] slots of a list are nonzero blocks; later slots are ignored. The count 12 occurs in every draw.
All inputs are finite; a program needn't handle non-finite values.
Results may differ from a plain program's by a relative error of at most 0.0055.
Values may be sent and summed in bfloat16 or wider, within the bound.
A program may use at most 64 MiB of HBM per device.

v0:
```python
import functools
import math

import jax
import jax.numpy as jnp
from jax import lax
from jax.experimental import pallas as pl
from jax.experimental.pallas import tpu as pltpu
from jax.sharding import PartitionSpec as P


def shards(features, col_panels, block_counts, block_values, weight, bias, cotangent):
    rep_count = lax.axis_size("rep")
    rep_index = lax.axis_index("rep")
    tile_size = block_values.shape[-1]
    feat_width = features.shape[1]
    own_panels = features.shape[0] // tile_size
    row_panels = col_panels.shape[0]
    slot_count = col_panels.shape[2]
    global_cols = col_panels[:, 0, :]
    local_cols = global_cols // (own_panels * rep_count) * own_panels + global_cols % own_panels
    live_counts = block_counts[:, 0]
    slot_mask = jnp.arange(slot_count, dtype=jnp.int32)[None, :] < live_counts[:, None]
    tiles = block_values[:, 0]
    empty = jnp.zeros((row_panels, tile_size, feat_width), jnp.float32)
    gathered = lax.all_gather(features, "section", axis=0, tiled=True)
    all_panels = gathered.reshape(-1, tile_size, feat_width)
    slot_step = 4
    turn_count = (jnp.max(live_counts) + slot_step - 1) // slot_step

    def one_turn(turn, running):
        begin_slot = turn * slot_step
        step_cols = lax.dynamic_slice_in_dim(local_cols, begin_slot, slot_step, 1)
        step_mask = lax.dynamic_slice_in_dim(slot_mask, begin_slot, slot_step, 1)
        step_tiles = lax.dynamic_slice_in_dim(tiles, begin_slot, slot_step, 1)
        step_tiles = jnp.where(step_mask[:, :, None, None], step_tiles, jnp.zeros((), jnp.bfloat16))
        picked = all_panels[step_cols]
        return running + jnp.einsum(
            "gkab,gkbf->gaf", step_tiles, picked, preferred_element_type=jnp.float32
        )

    gathered_sum = lax.fori_loop(0, turn_count, one_turn, empty)
    partial_value = gathered_sum.reshape(row_panels * tile_size, feat_width)
    own_rows = own_panels * tile_size
    summed_all = lax.psum(partial_value, "rep")
    summed_own = lax.dynamic_slice_in_dim(summed_all, rep_index * own_rows, own_rows, 0)
    aggregated = summed_own.astype(jnp.bfloat16)
    pre = jnp.dot(aggregated, weight, preferred_element_type=jnp.float32) + bias
    hidden = jax.nn.silu(pre).astype(jnp.bfloat16)
    sigmoid_pre = jax.nn.sigmoid(pre)
    slope = (
        cotangent.astype(jnp.float32) * (sigmoid_pre * (1.0 + pre * (1.0 - sigmoid_pre)))
    ).astype(jnp.bfloat16)
    local_weight = jnp.einsum("nd,nf->df", aggregated, slope, preferred_element_type=jnp.float32)
    local_bias = jnp.sum(slope.astype(jnp.float32), axis=0)
    weight_sum, bias_sum = lax.psum((local_weight, local_bias), ("section", "rep"))
    node_total = lax.axis_size("section") * rep_count * own_rows
    factor = 1.0 / math.sqrt(node_total)
    return (hidden, weight_sum * factor, bias_sum * factor)

MESH = pl.DeviceIdType.MESH
Z, PLANE = 4, 4
CHUNKS = 2


def fused_kernel(
    factor,
    feat, cols, counts, blocks, weight, bias, cot,
    hid_out, wg_out, bias_out,
    gath, dense, blk, wv, cotv, acc_own, acc_oth, acc_in, aggs, hidv,
    pair_out, pair_in, half32, half16, plane_in, sum32, sum16, line_in, fin,
    ext, ext_pair, ext_plane, ext_line,
    loc_sem, z_s, z_r, x_s, x_r, y_s, y_r, dx_s, dx_r, dy_s, dy_r,
    p_s, p_r, e_s, e_r, rs_s, rs_r, zl_s, zl_r, zg_s, zg_r, pg_s, pg_r, cg_s, cg_r,
):
    tile, width = feat.shape
    me, rep = lax.axis_index("section"), lax.axis_index("rep")
    z, q = me // PLANE, me % PLANE
    y, x = q // 2, q % 2

    def flip(j):
        return (1 - y if j & 2 else y) * 2 + (1 - x if j & 1 else x)

    def line(d):
        return lax.rem(z + d, Z)

    plane_peer = {j: (z * PLANE + flip(j), rep) for j in (1, 2, 3)}
    line_peer = {d: (line(d) * PLANE + q, rep) for d in (1, 2, 3)}
    core_peer = (me, 1 - rep)

    def remote(src, dst, send, recv, peer):
        return pltpu.make_async_remote_copy(
            src_ref=src, dst_ref=dst, send_sem=send, recv_sem=recv,
            device_id=peer, device_id_type=MESH,
        )

    own = gath.at[0, pl.ds(0, tile)]
    load_feat = pltpu.make_async_copy(feat, own, loc_sem.at[0])
    load_blk = pltpu.make_async_copy(blocks, blk, loc_sem.at[1])
    load_w = pltpu.make_async_copy(weight, wv, loc_sem.at[2])
    load_cot = pltpu.make_async_copy(cot, cotv, loc_sem.at[3])
    for c in (load_feat, load_blk, load_w, load_cot):
        c.start()

    barrier = pltpu.get_barrier_semaphore()
    peers = list(plane_peer.values()) + list(line_peer.values()) + [core_peer]
    for peer in peers:
        pl.semaphore_signal(barrier, inc=1, device_id=peer, device_id_type=MESH)
    pl.semaphore_wait(barrier, len(peers))
    load_feat.wait()

    def slot(j, k):
        return gath.at[j, pl.ds(pl.multiple_of(k * tile, tile), tile)]

    def half(j, k, h):
        part = tile // 2
        return gath.at[j, pl.ds(pl.multiple_of(k * tile + h * part, part), part)]

    first = 1 + 2 * (z // 2)
    second = 2 + z - 3 * (z // 2)
    order = (0, first, second, 6 - first - second)
    middle = (z + 1) // 2 == 1

    def pass_on(i, target):
        k = order[i]
        there = lax.rem(z + k - target + Z, Z)
        return remote(slot(0, k), slot(0, there), z_s.at[i], z_r.at[there], (target * PLANE + q, rep))

    up = remote(slot(0, 0), slot(0, Z - 1), z_s.at[0], z_r.at[Z - 1], ((z + 1) * PLANE + q, rep))
    down = remote(slot(0, 0), slot(0, 1), z_s.at[4], z_r.at[1], ((z - 1) * PLANE + q, rep))
    relay = {1: pass_on(1, lax.rem(3 * z + 1, Z)), 2: pass_on(2, Z - 1 - z), 3: pass_on(3, lax.rem(3 * z + 1, Z))}

    @pl.when(z < Z - 1)
    def _():
        up.start()

    @pl.when(z > 0)
    def _():
        down.start()

    x_copy = [remote(slot(0, k), slot(1, k), x_s.at[k], x_r.at[k], plane_peer[1]) for k in order]
    y_copy = [remote(slot(0, k), slot(2, k), y_s.at[k], y_r.at[k], plane_peer[2]) for k in order]
    dx_copy = [remote(half(2, k, 0), half(3, k, 0), dx_s.at[k], dx_r.at[k], plane_peer[1]) for k in order]
    dy_copy = [remote(half(1, k, 1), half(3, k, 1), dy_s.at[k], dy_r.at[k], plane_peer[2]) for k in order]
    x_copy[0].start()
    y_copy[0].start()

    def live(p):
        panel = rep if p == 0 else 1 - rep
        count = counts[panel]
        return [jnp.where(s < count, cols[panel, 0, s], -1) for s in range(cols.shape[2])]

    lists = [live(0), live(1)]
    load_blk.wait()
    for j in range(PLANE):
        for k in range(Z):
            for p in range(2):
                panel = rep if p == 0 else 1 - rep
                column = (line(k) * PLANE + flip(j)) * 2 + rep
                place = jnp.int32(0)
                for s, listed in enumerate(lists[p]):
                    place = jnp.where(listed == column, jnp.int32(s + 1), place)
                block = blk[panel, 0, jnp.maximum(place - 1, 0)]
                keep = jnp.minimum(place, 1).astype(jnp.float32).astype(jnp.bfloat16)
                dense[j, pl.ds(p * tile, tile), pl.ds(k * tile, tile)] = block * keep

    def forward(i):
        x_copy[i].wait_recv()
        dy_copy[i].start()
        y_copy[i].wait_recv()
        dx_copy[i].start()

    for i in (1, 2, 3):
        pltpu.make_async_copy(slot(0, 0), slot(0, order[i]), z_r.at[order[i]]).wait()

        @pl.when(middle)
        def _():
            relay[i].start()

        x_copy[i].start()
        y_copy[i].start()
        if i < 3:
            forward(i - 1)
    mine, theirs = pl.ds(0, tile), pl.ds(tile, tile)

    def product(j, part):
        return jnp.dot(dense[j, part], gath[j], preferred_element_type=jnp.float32)

    acc_own[...] = product(0, mine)
    acc_oth[...] = product(0, theirs)
    forward(2)
    forward(3)
    for j in (1, 2):
        acc_own[...] += product(j, mine)
        acc_oth[...] += product(j, theirs)
    for i in range(Z):
        dx_copy[i].wait_recv()
        dy_copy[i].wait_recv()
    acc_oth[...] += product(3, theirs)
    swap = remote(acc_oth, acc_in, p_s.at[0], p_r.at[0], core_peer)
    swap.start()
    acc_own[...] += product(3, mine)
    load_w.wait()
    load_cot.wait()
    swap.wait()

    agg = (acc_own[...] + acc_in[...]).astype(jnp.bfloat16)
    aggs[...] = agg
    pre = jnp.dot(agg, wv[...], preferred_element_type=jnp.float32) + bias[...]
    sig = jax.nn.sigmoid(pre)
    slope = (cotv[...].astype(jnp.float32) * (sig * (1.0 + pre * (1.0 - sig)))).astype(jnp.bfloat16)
    half_rows, columns = width // 2, width // CHUNKS
    quarter = half_rows // PLANE
    share = quarter // Z
    aligned = pl.multiple_of

    def grad_half(which, c):
        part = aggs[:, pl.ds(aligned(which * half_rows, half_rows), half_rows)]
        cut = slope[:, c * columns:(c + 1) * columns]
        return lax.dot_general(part, cut, (((0,), (0,)), ((), ())), preferred_element_type=jnp.float32)

    chunks = range(CHUNKS)
    pair = [remote(pair_out.at[c], pair_in.at[c], p_s.at[c + 2], p_r.at[c + 2], core_peer) for c in chunks]
    for c in chunks:
        pair_out[c] = grad_half(1 - rep, c).astype(jnp.bfloat16)
        pair[c].start()
    total = jnp.sum(slope.astype(jnp.float32), axis=0, keepdims=True)
    lanes = width // 4
    row_id = lax.broadcasted_iota(jnp.int32, (8, lanes), 0)
    spread = jnp.zeros((8, lanes), jnp.float32)
    for i in range(4):
        spread = jnp.where(row_id == i, total[:, i * lanes:(i + 1) * lanes], spread)
    ext[0] = spread
    ext_copy = remote(ext.at[0], ext_pair, p_s.at[1], p_r.at[1], core_peer)
    ext_copy.start()

    plane_sum = []
    for c in chunks:
        own_half = grad_half(rep, c)
        pair[c].wait_recv()
        both = own_half + pair_in[c].astype(jnp.float32)
        half32[c] = both
        half16[c] = both.astype(jnp.bfloat16)
        copies = []
        for j in (3, 1, 2):
            piece = half16.at[c, pl.ds(aligned(flip(j) * quarter, quarter), quarter)]
            copies.append(remote(piece, plane_in.at[c, j - 1], rs_s.at[c, j], rs_r.at[c, j], plane_peer[j]))
        for copy in copies:
            copy.start()
        plane_sum.append(copies)
    ext_copy.wait()
    ext[1] = ext[0] + ext_pair[...]
    ext_sum = [remote(ext.at[1], ext_plane.at[j - 1], e_s.at[j], e_r.at[j], plane_peer[j]) for j in (1, 2, 3)]
    for copy in ext_sum:
        copy.start()
    hidv[...] = (pre * sig).astype(jnp.bfloat16)
    store_hid = pltpu.make_async_copy(hidv, hid_out, loc_sem.at[4])
    store_hid.start()

    line_sum = []
    for c in chunks:
        for copy in plane_sum[c]:
            copy.wait_recv()
        part = half32[c, pl.ds(aligned(q * quarter, quarter), quarter)]
        for j in range(3):
            part = part + plane_in[c, j].astype(jnp.float32)
        sum32[c] = part
        sum16[c] = part.astype(jnp.bfloat16)
        copies = []
        for d in (2, 1, 3):
            piece = sum16.at[c, pl.ds(aligned(line(d) * share, share), share)]
            copies.append(remote(piece, line_in.at[c, Z - d - 1], zl_s.at[c, d], zl_r.at[c, Z - d], line_peer[d]))
        for copy in copies:
            copy.start()
        line_sum.append(copies)
    for copy in ext_sum:
        copy.wait()
    ext[2] = ext[1] + (ext_plane[0] + ext_plane[1] + ext_plane[2])
    ext_line_sum = [remote(ext.at[2], ext_line.at[Z - d - 1], e_s.at[d + 4], e_r.at[Z - d + 4], line_peer[d]) for d in (1, 2, 3)]
    for copy in ext_line_sum:
        copy.start()

    def region(c, core, place, height, count):
        start = core * half_rows + place * quarter + height * share
        return fin.at[c, pl.ds(aligned(start, share), count)]

    line_all = []
    for c in chunks:
        for copy in line_sum[c]:
            copy.wait_recv()
        part = sum32[c, pl.ds(aligned(z * share, share), share)]
        for d in range(3):
            part = part + line_in[c, d].astype(jnp.float32)
        here = region(c, rep, q, z, share)
        here[...] = part.astype(jnp.bfloat16)
        copies = [remote(here, here, zg_s.at[c, d], zg_r.at[c, Z - d], line_peer[d]) for d in (2, 1, 3)]
        for copy in copies:
            copy.start()
        line_all.append(copies)
    for copy in ext_line_sum:
        copy.wait()
    everything = ext[2] + (ext_line[0] + ext_line[1] + ext_line[2])
    for i in range(4):
        bias_out[:, i * lanes:(i + 1) * lanes] = everything[i:i + 1] * factor
    plane_all, core_all = [], []
    for c in chunks:
        for copy in line_all[c]:
            copy.wait_recv()
        own_q = region(c, rep, q, 0, quarter)
        copies = {j: remote(own_q, own_q, pg_s.at[c, j], pg_r.at[c, j], plane_peer[j]) for j in (3, 1, 2)}
        for copy in copies.values():
            copy.start()
        plane_all.append(copies)
        core_all.append(remote(own_q, own_q, cg_s.at[c, 0], cg_r.at[c, 0], core_peer))
        core_all[-1].start()
    for c in chunks:
        for j in (1, 2, 3):
            plane_all[c][j].wait_recv()
            piece = region(c, rep, flip(j), 0, quarter)
            core_all.append(remote(piece, piece, cg_s.at[c, j], cg_r.at[c, j], core_peer))
            core_all[-1].start()
    for copy in core_all:
        copy.wait()
    store_wg = []
    for c in chunks:
        store_wg.append(pltpu.make_async_copy(fin.at[c], wg_out.at[:, pl.ds(c * columns, columns)], loc_sem.at[5 + c]))
        store_wg[-1].start()
    for copies in plane_sum + line_sum + line_all + [list(p.values()) for p in plane_all] + [pair]:
        for copy in copies:
            copy.wait_send()

    for c in x_copy + y_copy + dx_copy + dy_copy:
        c.wait_send()

    @pl.when(z < Z - 1)
    def _():
        up.wait_send()

    @pl.when(z > 0)
    def _():
        down.wait_send()

    @pl.when(middle)
    def _():
        for c in relay.values():
            c.wait_send()

    store_hid.wait()
    for copy in store_wg:
        copy.wait()


def fused_shards(features, col_panels, block_counts, block_values, weight, bias, cotangent):
    tile, width = features.shape
    bf16, f32 = jnp.bfloat16, jnp.float32
    half_rows, columns = width // 2, width // CHUNKS
    quarter = half_rows // PLANE
    share = quarter // Z
    dma = pltpu.SemaphoreType.DMA
    hbm = pl.BlockSpec(memory_space=pl.ANY)

    smem = pl.BlockSpec(memory_space=pltpu.SMEM)
    vmem = pl.BlockSpec(memory_space=pltpu.VMEM)
    factor = 1.0 / math.sqrt(lax.axis_size("section") * lax.axis_size("rep") * tile)
    hidden, weight_sum, bias_sum = pl.pallas_call(
        functools.partial(fused_kernel, factor),
        out_shape=(
            jax.ShapeDtypeStruct((tile, width), bf16),
            jax.ShapeDtypeStruct((width, width), bf16),
            jax.ShapeDtypeStruct((1, width), f32),
        ),
        in_specs=[hbm, smem, smem, hbm, hbm, vmem, hbm],
        out_specs=(hbm, hbm, vmem),
        scratch_shapes=[
            pltpu.VMEM((PLANE, Z * tile, width), bf16),
            pltpu.VMEM((PLANE, 2 * tile, Z * tile), bf16),
            pltpu.VMEM(block_values.shape, bf16),
            pltpu.VMEM((width, width), bf16),
            pltpu.VMEM((tile, width), bf16),
            pltpu.VMEM((tile, width), f32),
            pltpu.VMEM((tile, width), f32),
            pltpu.VMEM((tile, width), f32),
            pltpu.VMEM((tile, width), bf16),
            pltpu.VMEM((tile, width), bf16),
            pltpu.VMEM((CHUNKS, half_rows, columns), bf16),
            pltpu.VMEM((CHUNKS, half_rows, columns), bf16),
            pltpu.VMEM((CHUNKS, half_rows, columns), f32),
            pltpu.VMEM((CHUNKS, half_rows, columns), bf16),
            pltpu.VMEM((CHUNKS, 3, quarter, columns), bf16),
            pltpu.VMEM((CHUNKS, quarter, columns), f32),
            pltpu.VMEM((CHUNKS, quarter, columns), bf16),
            pltpu.VMEM((CHUNKS, 3, share, columns), bf16),
            pltpu.VMEM((CHUNKS, width, columns), bf16),
            pltpu.VMEM((3, 8, width // 4), f32),
            pltpu.VMEM((8, width // 4), f32),
            pltpu.VMEM((3, 8, width // 4), f32),
            pltpu.VMEM((3, 8, width // 4), f32),
            dma((5 + CHUNKS,)),
            dma((5,)), dma((4,)), dma((4,)), dma((4,)), dma((4,)), dma((4,)),
            dma((4,)), dma((4,)), dma((4,)), dma((4,)),
            dma((2 + CHUNKS,)), dma((2 + CHUNKS,)), dma((8,)), dma((8,)),
        ] + [dma((CHUNKS, 4))] * 10,
        compiler_params=pltpu.CompilerParams(
            collective_id=0, has_side_effects=True, vmem_limit_bytes=60 * 1024 * 1024
        ),
        name="fused_layer",
    )(features, col_panels, block_counts.reshape(-1), block_values, weight, bias.reshape(1, width), cotangent)
    return hidden, weight_sum.astype(f32) * factor, bias_sum[0]


def fits_fused(mesh):
    return dict(mesh.shape) == {"section": Z * PLANE, "rep": 2}


def solution(mesh):
    in_specs = (
        P(("section", "rep"), None),
        P("section", "rep", None),
        P("section", "rep"),
        P("section", "rep", None, None, None),
        P(),
        P(),
        P(("section", "rep"), None),
    )
    out_specs = (P(("section", "rep"), None), P(), P())
    body = fused_shards if fits_fused(mesh) else shards
    return jax.shard_map(body, mesh=mesh, in_specs=in_specs, out_specs=out_specs, check_vma=False)
```

profile of v0, /device:TPU:0, one launch (start us, length us, event | category | flops | bytes accessed | tf_op | source)
XLA Modules:
  0.0 54.1 jit_solution(381361436636366100)
XLA Ops:
  0.6 50.0 %fused_layer.1 = (bf16[128,512]{1,0:T(8,128)(2,1)}, bf16[512,512]{1,0:T(8,128)(2,1)}, f32[1,512]{1,0:T(1,128)}) custom-call(bf16[128,512]{1,0:T(8,128)(2,1)} %feat.1, s32[2,1,12]{2,1,0:T(1,128)} %cols.1, s32[2]{0:T(128)} %bitcast.5, bf16[2,1,12,128,128]{4,3,2,1,0:T(8,128)(2,1)} %blocks.1, bf16[512,512]{1,0:T(8,128)(2,1)} %weight.1, f32[1,512]{1,0:T(1,128)} %bitcast.3, ...), custom_call_target="tpu_custom_call" | custom-call | tf_op jit(solution)/shard_map/fused_layer/pallas_call | solution.py:365
  50.7 0.0 copy-start
  50.7 2.2 %convert_multiply_fusion = f32[512,512]{1,0:T(8,128)} fusion(bf16[512,512]{1,0:T(8,128)(2,1)} %get-tuple-element.7), kind=kLoop, calls=%fused_computation | loop fusion | flops 524288 | bytes 1572864 | tf_op jit(solution)/shard_map/mul | solution.py:408
  52.9 0.0 copy-done
  52.9 0.0 copy-start.1
  52.9 0.7 %copy.12 = bf16[128,512]{1,0:T(8,128)(2,1)} copy(bf16[128,512]{1,0:T(8,128)(2,1)S(1)} %copy-done) | data formatting | bytes 262144
  53.5 0.0 copy-done.1
  53.6 0.6 %copy.13 = f32[512]{0:T(512)} copy(f32[512]{0:T(512)S(1)} %bitcast.4) | data formatting | bytes 4096
Async XLA Ops:
  50.7 2.2 %copy-start = (bf16[128,512]{1,0:T(8,128)(2,1)S(1)}, bf16[128,512]{1,0:T(8,128)(2,1)}, u32[]{:S(2)}) copy-start(bf16[128,512]{1,0:T(8,128)(2,1)} %get-tuple-element.12) | copy-start | bytes 393220
  52.9 0.7 %copy-start.1 = (f32[1,512]{1,0:T(1,128)S(1)}, f32[1,512]{1,0:T(1,128)}, u32[]{:S(2)}) copy-start(f32[1,512]{1,0:T(1,128)} %get-tuple-element.8) | copy-start | bytes 6148
where the time goes:
time: 54.3 us; the launch traced here: 54.1 us
  Pallas kernels  50 us (92%)
  other arithmetic  2.19 us (4%)
  local copies, waits for them, and re-layouts  1.25 us (2%)
  between operations  0.65 us (1%)
    pallas_call x1, Pallas kernels, fused_shards(): pl.pallas_call(functools.partial(fused_kernel, factor), out_shape=(jax.Sh...  50 us
    mul x1, other arithmetic, fused_shards(): return (hidden, weight_sum.astype(f32) * factor, bias_sum[0])  2.19 us
    unnamed x6, local copies, waits for them, and re-layouts  1.25 us

commit v1 on v0

--- a/solution.py
+++ b/solution.py
@@ -121,25 +121,51 @@
     order = (0, first, second, 6 - first - second)
     middle = (z + 1) // 2 == 1
 
-    def pass_on(i, target):
+    cross = tile - tile // 4
+
+    def piece(j, k):
+        start, count = (0, tile) if j == 0 else (cross, tile - cross)
+        return gath.at[j, pl.ds(pl.multiple_of(k * tile + start, 16), count)]
+
+    def head(j, k):
+        return gath.at[j, pl.ds(pl.multiple_of(k * tile, tile), cross)]
+
+    def pass_on(j, i, target):
         k = order[i]
         there = lax.rem(z + k - target + Z, Z)
-        return remote(slot(0, k), slot(0, there), z_s.at[i], z_r.at[there], (target * PLANE + q, rep))
-
-    up = remote(slot(0, 0), slot(0, Z - 1), z_s.at[0], z_r.at[Z - 1], ((z + 1) * PLANE + q, rep))
-    down = remote(slot(0, 0), slot(0, 1), z_s.at[4], z_r.at[1], ((z - 1) * PLANE + q, rep))
-    relay = {1: pass_on(1, lax.rem(3 * z + 1, Z)), 2: pass_on(2, Z - 1 - z), 3: pass_on(3, lax.rem(3 * z + 1, Z))}
-
-    @pl.when(z < Z - 1)
-    def _():
-        up.start()
-
-    @pl.when(z > 0)
-    def _():
-        down.start()
-
-    x_copy = [remote(slot(0, k), slot(1, k), x_s.at[k], x_r.at[k], plane_peer[1]) for k in order]
-    y_copy = [remote(slot(0, k), slot(2, k), y_s.at[k], y_r.at[k], plane_peer[2]) for k in order]
+        return remote(piece(j, k), piece(j, there), z_s.at[j, i], z_r.at[j, there], (target * PLANE + q, rep))
+
+    up = [remote(piece(j, 0), piece(j, Z - 1), z_s.at[j, 0], z_r.at[j, Z - 1], ((z + 1) * PLANE + q, rep)) for j in range(3)]
+    down = [remote(piece(j, 0), piece(j, 1), z_s.at[j, 4], z_r.at[j, 1], ((z - 1) * PLANE + q, rep)) for j in range(3)]
+    outer, inner = lax.rem(3 * z + 1, Z), Z - 1 - z
+    relay = [{1: pass_on(j, 1, outer), 2: pass_on(j, 2, inner), 3: pass_on(j, 3, outer)} for j in range(3)]
+
+    def send_along(j):
+        @pl.when(z < Z - 1)
+        def _():
+            up[j].start()
+
+        @pl.when(z > 0)
+        def _():
+            down[j].start()
+
+    def relay_along(j, i):
+        pltpu.make_async_copy(piece(j, 0), piece(j, order[i]), z_r.at[j, order[i]]).wait()
+
+        @pl.when(middle)
+        def _():
+            relay[j][i].start()
+
+    send_along(0)
+
+    def across(j, i):
+        k = order[i]
+        send, recv = ((x_s, x_r), (y_s, y_r))[j - 1]
+        part = slot if i == 0 else head
+        return remote(part(0, k), part(j, k), send.at[k], recv.at[k], plane_peer[j])
+
+    x_copy = [across(1, i) for i in range(Z)]
+    y_copy = [across(2, i) for i in range(Z)]
     dx_copy = [remote(half(2, k, 0), half(3, k, 0), dx_s.at[k], dx_r.at[k], plane_peer[1]) for k in order]
     dy_copy = [remote(half(1, k, 1), half(3, k, 1), dy_s.at[k], dy_r.at[k], plane_peer[2]) for k in order]
     x_copy[0].start()
@@ -165,18 +191,21 @@
                 dense[j, pl.ds(p * tile, tile), pl.ds(k * tile, tile)] = block * keep
 
     def forward(i):
+        y_copy[i].wait_recv()
+        if i == 0:
+            send_along(2)
+        dx_copy[i].start()
         x_copy[i].wait_recv()
+        if i == 0:
+            send_along(1)
+        else:
+            relay_along(1, i)
         dy_copy[i].start()
-        y_copy[i].wait_recv()
-        dx_copy[i].start()
+        if i:
+            relay_along(2, i)
 
     for i in (1, 2, 3):
-        pltpu.make_async_copy(slot(0, 0), slot(0, order[i]), z_r.at[order[i]]).wait()
-
-        @pl.when(middle)
-        def _():
-            relay[i].start()
-
+        relay_along(0, i)
         x_copy[i].start()
         y_copy[i].start()
         if i < 3:
@@ -334,16 +363,19 @@
 
     @pl.when(z < Z - 1)
     def _():
-        up.wait_send()
+        for c in up:
+            c.wait_send()
 
     @pl.when(z > 0)
     def _():
-        down.wait_send()
+        for c in down:
+            c.wait_send()
 
     @pl.when(middle)
     def _():
-        for c in relay.values():
-            c.wait_send()
+        for j in range(3):
+            for c in relay[j].values():
+                c.wait_send()
 
     store_hid.wait()
     for copy in store_wg:
@@ -396,7 +428,7 @@
             pltpu.VMEM((3, 8, width // 4), f32),
             pltpu.VMEM((3, 8, width // 4), f32),
             dma((5 + CHUNKS,)),
-            dma((5,)), dma((4,)), dma((4,)), dma((4,)), dma((4,)), dma((4,)),
+            dma((3, 5)), dma((3, 4)), dma((4,)), dma((4,)), dma((4,)), dma((4,)),
             dma((4,)), dma((4,)), dma((4,)), dma((4,)),
             dma((2 + CHUNKS,)), dma((2 + CHUNKS,)), dma((8,)), dma((8,)),
         ] + [dma((CHUNKS, 4))] * 10,

time: 54.3 us -> 55.2 us (1.017)
  Pallas kernels: 50 us -> 50.9 us
    pallas_call x1, Pallas kernels: 50 us -> 50.9 us  [fused_shards(): pl.pallas_call(functools.partial(fused_kernel, factor), out_shape=(jax.Sh...]
where the time goes in v1:
time: 55.2 us; the launch traced here: 55 us
  Pallas kernels  50.9 us (92%)
  other arithmetic  2.19 us (4%)
  local copies, waits for them, and re-layouts  1.25 us (2%)
  between operations  0.65 us (1%)
    pallas_call x1, Pallas kernels, fused_shards(): pl.pallas_call(functools.partial(fused_kernel, factor), out_shape=(jax.Sh...  50.9 us
    mul x1, other arithmetic, fused_shards(): return (hidden, weight_sum.astype(f32) * factor, bias_sum[0])  2.19 us
    unnamed x6, local copies, waits for them, and re-layouts  1.25 us

profile of v1, /device:TPU:0, one launch (start us, length us, event | category | flops | bytes accessed | tf_op | source)
XLA Modules:
  0.0 55.0 jit_solution(11699196976241136497)
XLA Ops:
  0.6 50.9 %fused_layer.1 = (bf16[128,512]{1,0:T(8,128)(2,1)}, bf16[512,512]{1,0:T(8,128)(2,1)}, f32[1,512]{1,0:T(1,128)}) custom-call(bf16[128,512]{1,0:T(8,128)(2,1)} %feat.1, s32[2,1,12]{2,1,0:T(1,128)} %cols.1, s32[2]{0:T(128)} %bitcast.5, bf16[2,1,12,128,128]{4,3,2,1,0:T(8,128)(2,1)} %blocks.1, bf16[512,512]{1,0:T(8,128)(2,1)} %weight.1, f32[1,512]{1,0:T(1,128)} %bitcast.3, ...), custom_call_target="tpu_custom_call" | custom-call | tf_op jit(solution)/shard_map/fused_layer/pallas_call | solution.py:397
  51.5 0.0 copy-start
  51.6 2.2 %convert_multiply_fusion = f32[512,512]{1,0:T(8,128)} fusion(bf16[512,512]{1,0:T(8,128)(2,1)} %get-tuple-element.7), kind=kLoop, calls=%fused_computation | loop fusion | flops 524288 | bytes 1572864 | tf_op jit(solution)/shard_map/mul | solution.py:440
  53.7 0.0 copy-done
  53.7 0.0 copy-start.1
  53.7 0.7 %copy.12 = bf16[128,512]{1,0:T(8,128)(2,1)} copy(bf16[128,512]{1,0:T(8,128)(2,1)S(1)} %copy-done) | data formatting | bytes 262144
  54.4 0.0 copy-done.1
  54.4 0.6 %copy.13 = f32[512]{0:T(512)} copy(f32[512]{0:T(512)S(1)} %bitcast.4) | data formatting | bytes 4096
Async XLA Ops:
  51.5 2.2 %copy-start = (bf16[128,512]{1,0:T(8,128)(2,1)S(1)}, bf16[128,512]{1,0:T(8,128)(2,1)}, u32[]{:S(2)}) copy-start(bf16[128,512]{1,0:T(8,128)(2,1)} %get-tuple-element.12) | copy-start | bytes 393220
  53.7 0.7 %copy-start.1 = (f32[1,512]{1,0:T(1,128)S(1)}, f32[1,512]{1,0:T(1,128)}, u32[]{:S(2)}) copy-start(f32[1,512]{1,0:T(1,128)} %get-tuple-element.8) | copy-start | bytes 6148

commit v2 on v0

--- a/solution.py
+++ b/solution.py
@@ -121,30 +121,37 @@
     order = (0, first, second, 6 - first - second)
     middle = (z + 1) // 2 == 1
 
-    def pass_on(i, target):
+    def pass_on(i, h, target):
         k = order[i]
         there = lax.rem(z + k - target + Z, Z)
-        return remote(slot(0, k), slot(0, there), z_s.at[i], z_r.at[there], (target * PLANE + q, rep))
-
-    up = remote(slot(0, 0), slot(0, Z - 1), z_s.at[0], z_r.at[Z - 1], ((z + 1) * PLANE + q, rep))
-    down = remote(slot(0, 0), slot(0, 1), z_s.at[4], z_r.at[1], ((z - 1) * PLANE + q, rep))
-    relay = {1: pass_on(1, lax.rem(3 * z + 1, Z)), 2: pass_on(2, Z - 1 - z), 3: pass_on(3, lax.rem(3 * z + 1, Z))}
-
-    @pl.when(z < Z - 1)
-    def _():
-        up.start()
-
-    @pl.when(z > 0)
-    def _():
-        down.start()
-
-    x_copy = [remote(slot(0, k), slot(1, k), x_s.at[k], x_r.at[k], plane_peer[1]) for k in order]
-    y_copy = [remote(slot(0, k), slot(2, k), y_s.at[k], y_r.at[k], plane_peer[2]) for k in order]
+        return remote(half(0, k, h), half(0, there, h), z_s.at[h, i], z_r.at[h, there], (target * PLANE + q, rep))
+
+    up = [remote(half(0, 0, h), half(0, Z - 1, h), z_s.at[h, 0], z_r.at[h, Z - 1], ((z + 1) * PLANE + q, rep)) for h in range(2)]
+    down = [remote(half(0, 0, h), half(0, 1, h), z_s.at[h, 4], z_r.at[h, 1], ((z - 1) * PLANE + q, rep)) for h in range(2)]
+    outer, inner = lax.rem(3 * z + 1, Z), Z - 1 - z
+    relay = [{1: pass_on(1, h, outer), 2: pass_on(2, h, inner), 3: pass_on(3, h, outer)} for h in range(2)]
+
+    def across(j, i, h):
+        k = order[i]
+        send, recv = ((x_s, x_r), (y_s, y_r))[j - 1]
+        return remote(half(0, k, h), half(j, k, h), send.at[h, k], recv.at[h, k], plane_peer[j])
+
+    x_copy = [[across(1, i, h) for h in range(2)] for i in range(Z)]
+    y_copy = [[across(2, i, h) for h in range(2)] for i in range(Z)]
+    for h in range(2):
+        x_copy[0][1 - h].start()
+        y_copy[0][h].start()
+
+        @pl.when(z < Z - 1)
+        def _():
+            up[h].start()
+
+        @pl.when(z > 0)
+        def _():
+            down[h].start()
+
     dx_copy = [remote(half(2, k, 0), half(3, k, 0), dx_s.at[k], dx_r.at[k], plane_peer[1]) for k in order]
     dy_copy = [remote(half(1, k, 1), half(3, k, 1), dy_s.at[k], dy_r.at[k], plane_peer[2]) for k in order]
-    x_copy[0].start()
-    y_copy[0].start()
-
     def live(p):
         panel = rep if p == 0 else 1 - rep
         count = counts[panel]
@@ -165,41 +172,51 @@
                 dense[j, pl.ds(p * tile, tile), pl.ds(k * tile, tile)] = block * keep
 
     def forward(i):
-        x_copy[i].wait_recv()
+        x_copy[i][1].wait_recv()
         dy_copy[i].start()
-        y_copy[i].wait_recv()
+        y_copy[i][0].wait_recv()
         dx_copy[i].start()
 
     for i in (1, 2, 3):
-        pltpu.make_async_copy(slot(0, 0), slot(0, order[i]), z_r.at[order[i]]).wait()
-
-        @pl.when(middle)
-        def _():
-            relay[i].start()
-
-        x_copy[i].start()
-        y_copy[i].start()
-        if i < 3:
-            forward(i - 1)
+        for h in range(2):
+            k = order[i]
+            pltpu.make_async_copy(half(0, 0, h), half(0, k, h), z_r.at[h, k]).wait()
+
+            @pl.when(middle)
+            def _():
+                relay[h][i].start()
+
+            (y_copy if h == 0 else x_copy)[i][h].start()
+        x_copy[i][0].start()
+        y_copy[i][1].start()
+        forward(i - 1)
     mine, theirs = pl.ds(0, tile), pl.ds(tile, tile)
 
     def product(j, part):
         return jnp.dot(dense[j, part], gath[j], preferred_element_type=jnp.float32)
 
+    def corner(i, part):
+        at = pl.ds(pl.multiple_of(order[i] * tile, tile), tile)
+        return jnp.dot(dense[3, part, at], gath[3, at], preferred_element_type=jnp.float32)
+
     acc_own[...] = product(0, mine)
     acc_oth[...] = product(0, theirs)
-    forward(2)
     forward(3)
+    for i in range(Z):
+        x_copy[i][0].wait_recv()
+        y_copy[i][1].wait_recv()
     for j in (1, 2):
         acc_own[...] += product(j, mine)
         acc_oth[...] += product(j, theirs)
     for i in range(Z):
         dx_copy[i].wait_recv()
         dy_copy[i].wait_recv()
-    acc_oth[...] += product(3, theirs)
+        acc_oth[...] += corner(i, theirs)
+        if i < Z - 1:
+            acc_own[...] += corner(i, mine)
     swap = remote(acc_oth, acc_in, p_s.at[0], p_r.at[0], core_peer)
     swap.start()
-    acc_own[...] += product(3, mine)
+    acc_own[...] += corner(Z - 1, mine)
     load_w.wait()
     load_cot.wait()
     swap.wait()
@@ -329,20 +346,22 @@
         for copy in copies:
             copy.wait_send()
 
-    for c in x_copy + y_copy + dx_copy + dy_copy:
+    for c in sum(x_copy + y_copy, []) + dx_copy + dy_copy:
         c.wait_send()
 
     @pl.when(z < Z - 1)
     def _():
-        up.wait_send()
+        for c in up:
+            c.wait_send()
 
     @pl.when(z > 0)
     def _():
-        down.wait_send()
+        for c in down:
+            c.wait_send()
 
     @pl.when(middle)
     def _():
-        for c in relay.values():
+        for c in list(relay[0].values()) + list(relay[1].values()):
             c.wait_send()
 
     store_hid.wait()
@@ -396,7 +415,7 @@
             pltpu.VMEM((3, 8, width // 4), f32),
             pltpu.VMEM((3, 8, width // 4), f32),
             dma((5 + CHUNKS,)),
-            dma((5,)), dma((4,)), dma((4,)), dma((4,)), dma((4,)), dma((4,)),
+            dma((2, 5)), dma((2, 4)), dma((2, 4)), dma((2, 4)), dma((2, 4)), dma((2, 4)),
             dma((4,)), dma((4,)), dma((4,)), dma((4,)),
             dma((2 + CHUNKS,)), dma((2 + CHUNKS,)), dma((8,)), dma((8,)),
         ] + [dma((CHUNKS, 4))] * 10,

time: 54.3 us -> 53.8 us (level)
  no operation moved by 1% of the time
where the time goes in v2:
time: 53.8 us; the launch traced here: 53.6 us
  Pallas kernels  49.5 us (92%)
  other arithmetic  2.19 us (4%)
  local copies, waits for them, and re-layouts  1.25 us (2%)
  between operations  0.65 us (1%)
    pallas_call x1, Pallas kernels, fused_shards(): pl.pallas_call(functools.partial(fused_kernel, factor), out_shape=(jax.Sh...  49.5 us
    mul x1, other arithmetic, fused_shards(): return (hidden, weight_sum.astype(f32) * factor, bias_sum[0])  2.19 us
    unnamed x6, local copies, waits for them, and re-layouts  1.25 us

profile of v2, /device:TPU:0, one launch (start us, length us, event | category | flops | bytes accessed | tf_op | source)
XLA Modules:
  0.0 53.6 jit_solution(12866028483324493416)
XLA Ops:
  0.6 49.5 %fused_layer.1 = (bf16[128,512]{1,0:T(8,128)(2,1)}, bf16[512,512]{1,0:T(8,128)(2,1)}, f32[1,512]{1,0:T(1,128)}) custom-call(bf16[128,512]{1,0:T(8,128)(2,1)} %feat.1, s32[2,1,12]{2,1,0:T(1,128)} %cols.1, s32[2]{0:T(128)} %bitcast.5, bf16[2,1,12,128,128]{4,3,2,1,0:T(8,128)(2,1)} %blocks.1, bf16[512,512]{1,0:T(8,128)(2,1)} %weight.1, f32[1,512]{1,0:T(1,128)} %bitcast.3, ...), custom_call_target="tpu_custom_call" | custom-call | tf_op jit(solution)/shard_map/fused_layer/pallas_call | solution.py:384
  50.2 0.0 copy-start
  50.2 2.2 %convert_multiply_fusion = f32[512,512]{1,0:T(8,128)} fusion(bf16[512,512]{1,0:T(8,128)(2,1)} %get-tuple-element.7), kind=kLoop, calls=%fused_computation | loop fusion | flops 524288 | bytes 1572864 | tf_op jit(solution)/shard_map/mul | solution.py:427
  52.4 0.0 copy-done
  52.4 0.0 copy-start.1
  52.4 0.7 %copy.12 = bf16[128,512]{1,0:T(8,128)(2,1)} copy(bf16[128,512]{1,0:T(8,128)(2,1)S(1)} %copy-done) | data formatting | bytes 262144
  53.0 0.0 copy-done.1
  53.0 0.6 %copy.13 = f32[512]{0:T(512)} copy(f32[512]{0:T(512)S(1)} %bitcast.4) | data formatting | bytes 4096
Async XLA Ops:
  50.2 2.2 %copy-start = (bf16[128,512]{1,0:T(8,128)(2,1)S(1)}, bf16[128,512]{1,0:T(8,128)(2,1)}, u32[]{:S(2)}) copy-start(bf16[128,512]{1,0:T(8,128)(2,1)} %get-tuple-element.12) | copy-start | bytes 393220
  52.4 0.7 %copy-start.1 = (f32[1,512]{1,0:T(1,128)S(1)}, f32[1,512]{1,0:T(1,128)}, u32[]{:S(2)}) copy-start(f32[1,512]{1,0:T(1,128)} %get-tuple-element.8) | copy-start | bytes 6148

commit v3 on v2

--- a/solution.py
+++ b/solution.py
@@ -60,7 +60,7 @@
 
 MESH = pl.DeviceIdType.MESH
 Z, PLANE = 4, 4
-CHUNKS = 2
+CHUNKS = 4
 
 
 def fused_kernel(

time: 53.8 us -> 54.2 us (level)
  no operation moved by 1% of the time
where the time goes in v3:
time: 54.2 us; the launch traced here: 54 us
  Pallas kernels  49.9 us (92%)
  other arithmetic  2.19 us (4%)
  local copies, waits for them, and re-layouts  1.25 us (2%)
  between operations  0.65 us (1%)
    pallas_call x1, Pallas kernels, fused_shards(): pl.pallas_call(functools.partial(fused_kernel, factor), out_shape=(jax.Sh...  49.9 us
    mul x1, other arithmetic, fused_shards(): return (hidden, weight_sum.astype(f32) * factor, bias_sum[0])  2.19 us
    unnamed x6, local copies, waits for them, and re-layouts  1.25 us

profile of v3, /device:TPU:0, one launch (start us, length us, event | category | flops | bytes accessed | tf_op | source)
XLA Modules:
  0.0 54.0 jit_solution(14476036462393105078)
XLA Ops:
  0.6 49.9 %fused_layer.1 = (bf16[128,512]{1,0:T(8,128)(2,1)}, bf16[512,512]{1,0:T(8,128)(2,1)}, f32[1,512]{1,0:T(1,128)}) custom-call(bf16[128,512]{1,0:T(8,128)(2,1)} %feat.1, s32[2,1,12]{2,1,0:T(1,128)} %cols.1, s32[2]{0:T(128)} %bitcast.5, bf16[2,1,12,128,128]{4,3,2,1,0:T(8,128)(2,1)} %blocks.1, bf16[512,512]{1,0:T(8,128)(2,1)} %weight.1, f32[1,512]{1,0:T(1,128)} %bitcast.3, ...), custom_call_target="tpu_custom_call" | custom-call | tf_op jit(solution)/shard_map/fused_layer/pallas_call | solution.py:384
  50.6 0.0 copy-start
  50.6 2.2 %convert_multiply_fusion = f32[512,512]{1,0:T(8,128)} fusion(bf16[512,512]{1,0:T(8,128)(2,1)} %get-tuple-element.7), kind=kLoop, calls=%fused_computation | loop fusion | flops 524288 | bytes 1572864 | tf_op jit(solution)/shard_map/mul | solution.py:427
  52.8 0.0 copy-done
  52.8 0.0 copy-start.1
  52.8 0.7 %copy.12 = bf16[128,512]{1,0:T(8,128)(2,1)} copy(bf16[128,512]{1,0:T(8,128)(2,1)S(1)} %copy-done) | data formatting | bytes 262144
  53.4 0.0 copy-done.1
  53.4 0.6 %copy.13 = f32[512]{0:T(512)} copy(f32[512]{0:T(512)S(1)} %bitcast.4) | data formatting | bytes 4096
Async XLA Ops:
  50.6 2.2 %copy-start = (bf16[128,512]{1,0:T(8,128)(2,1)S(1)}, bf16[128,512]{1,0:T(8,128)(2,1)}, u32[]{:S(2)}) copy-start(bf16[128,512]{1,0:T(8,128)(2,1)} %get-tuple-element.12) | copy-start | bytes 393220
  52.8 0.7 %copy-start.1 = (f32[1,512]{1,0:T(1,128)S(1)}, f32[1,512]{1,0:T(1,128)}, u32[]{:S(2)}) copy-start(f32[1,512]{1,0:T(1,128)} %get-tuple-element.8) | copy-start | bytes 6148
